TPU v7x, 512 devices: a whole 4x4x16 slice. The times are simulated.
512 devices in a mesh: replica: 64 (over x, z), tensor: 8 (over y, core).
Axes of the slice: x: 4, y: 4, z: 16, core: 2. Of those that a mesh axis runs over, the one named last changes fastest.
Arguments:
- suffix_x: bfloat16 [16384, 8192], P('replica', 'tensor'), may hold values from -6 to 6
- suffix_z: bfloat16 [16384, 8192], P('replica', 'tensor'), may hold values from -6 to 6
- suffix_b: bfloat16 [16384, 2048], P('replica', 'tensor'), may hold values from -1.5 to 1.5
- suffix_c: bfloat16 [16384, 2048], P('replica', 'tensor'), may hold values from -1.5 to 1.5
- suffix_dt: float32 [16384, 128], P('replica', 'tensor'), may hold values from -3 to 15
- missed_x: bfloat16 [49152, 8192], P('replica', 'tensor'), may hold values from -6 to 6
- missed_b: bfloat16 [49152, 2048], P('replica', 'tensor'), may hold values from -1.5 to 1.5
- missed_dt: float32 [49152, 128], P('replica', 'tensor'), may hold values from -3 to 15
- dt_bias: float32 [128], P('tensor'), may hold values from -1 to 1
- a_log: float32 [128], P('tensor'), may hold values from -8 to -2
- skip_weight_per_head: float32 [128], P('tensor'), may hold values from 0.5 to 2
- norm_gain: float32 [8192], P('tensor'), may hold values from 0.1 to 1.9
- out_weight: bfloat16 [8192, 4096], P('tensor', 'replica'), may hold values from -0.1875 to 0.1875
- cache_pages: bfloat16 [3072, 8, 32, 256], P('replica', 'tensor'), may hold values from -12 to 12
- hit_holder: int32 [8, 128, 32, 1], P('tensor'), may hold values from 0 to 63; in each aligned block of 64 rows (0 to 63, 64 to 127, ..., all dimensions but the last counted through in order) at most 2 rows name the same one
- hit_slot: int32 [8, 128, 32], P('tensor'), may hold values from 0 to 47
- missed: int32 [128], P('replica'), may hold values from 0 to 3, as said below
Outputs:
- mixed: bfloat16 [16384, 4096], P('replica', 'tensor')
Inputs may be any that keep to these rules, and one draw needn't show every extreme that they name: `hit_holder`: among the pages of the 2 requests r * 2 .. r * 2 + 1 in one set of heads, at most 2 name the same holder, and in each draw some holder is named by exactly 2 of them. `missed`: some request misses all 3 blocks in every draw.
All inputs are finite; a program needn't handle non-finite values.
Results may differ from a plain program's by a relative error of at most 0.017.
Values may be sent and summed in bfloat16 or wider, within the bound.
A program may use at most 64 MiB of HBM per device.

v0:
```python
import jax
import jax.numpy as jnp
from jax import lax
from jax.sharding import PartitionSpec as P

P_SIZE = 64
N = 256
SPAN = 128
MISS_MAX = 3


def state_update(span_x, span_b, step_size, log_decay, prior):
    req_count, length, head_count, head_width = span_x.shape
    groups = span_b.shape[2]
    cumulative = jnp.cumsum(log_decay, axis=1)
    span_total = cumulative[:, -1]
    weight_matrix = jnp.exp(span_total[:, None, :] - cumulative) * step_size
    scaled = (span_x * weight_matrix[..., None]).astype(jnp.bfloat16)
    scaled = scaled.reshape(req_count, length, groups, head_count // groups, head_width)
    gained = jnp.einsum("rlgkp,rlgn->rgkpn", scaled, span_b, preferred_element_type=jnp.float32)
    return jnp.exp(span_total)[:, :, None, None] * prior + gained.reshape(
        req_count, head_count, head_width, -1
    )


def span_output(span_x, span_b, span_c, step_size, log_decay, prior, skip_weight_per_head):
    req_count, length, head_count, head_width = span_x.shape
    groups = span_b.shape[2]
    per_group = head_count // groups
    cumulative = jnp.cumsum(log_decay, axis=1)
    scores = jnp.einsum("rlgn,rsgn->rlsg", span_c, span_b, preferred_element_type=jnp.float32)
    positions = jnp.arange(length)
    causal = positions[:, None] >= positions[None, :]
    logarithmic_spacing = jnp.where(
        causal[None, :, :, None], cumulative[:, :, None, :] - cumulative[:, None, :, :], -jnp.inf
    )
    mixing = jnp.exp(logarithmic_spacing) * step_size[:, None, :, :]
    mixing = (
        mixing.reshape(req_count, length, length, groups, per_group) * scores[..., None]
    ).astype(jnp.bfloat16)
    grouped_x = span_x.reshape(req_count, length, groups, per_group, head_width)
    inner_part = jnp.einsum(
        "rlsgk,rsgkp->rlgkp", mixing, grouped_x, preferred_element_type=jnp.float32
    )
    carried = jnp.einsum(
        "rlgn,rgkpn->rlgkp",
        span_c.astype(jnp.float32),
        prior.reshape(req_count, groups, per_group, head_width, -1),
        precision=lax.Precision.HIGHEST,
    )
    carried = carried * jnp.exp(cumulative).reshape(req_count, length, groups, per_group)[..., None]
    skipped = skip_weight_per_head.reshape(groups, per_group)[:, :, None] * grouped_x.astype(
        jnp.float32
    )
    return (inner_part + carried + skipped).reshape(req_count * length, head_count * head_width)


def gate_norm(values, gate_in, norm_scale, groups):
    length = values.shape[0]
    gated = values * jax.nn.silu(gate_in.astype(jnp.float32))
    grouped = gated.reshape(length, groups, -1)
    reciprocal_root_mean = lax.rsqrt(jnp.mean(grouped * grouped, axis=-1, keepdims=True) + 1e-05)
    return ((grouped * reciprocal_root_mean).reshape(length, -1) * norm_scale).astype(jnp.bfloat16)


def per_device(
    suffix_x,
    suffix_z,
    suffix_b,
    suffix_c,
    suffix_dt,
    missed_x,
    missed_b,
    missed_dt,
    dt_bias,
    a_log,
    skip_weight_per_head,
    norm_gain,
    out_weight,
    cache_pages,
    hit_holder,
    hit_slot,
    missed,
):
    owners = lax.axis_size("replica")
    self_index = lax.axis_index("replica")
    req_here = missed.shape[0]
    heads_here = dt_bias.shape[0]
    groups_here = suffix_b.shape[1] // N
    hit_rows = hit_holder.shape[1] * hit_holder.shape[2] // owners
    slot_limit = max(2, 2 * hit_rows // owners)
    holders = hit_holder[0, :, :, 0].reshape(owners, hit_rows)
    slot_ids = hit_slot[0].reshape(owners, hit_rows)
    positions = jnp.arange(hit_rows)
    earlier = (holders[:, :, None] == holders[:, None, :]) & (
        positions[None, None, :] < positions[None, :, None]
    )
    ranks = jnp.sum(earlier, axis=2, dtype=jnp.int32)
    wanted = (holders == self_index)[:, None, :] & (
        ranks[:, None, :] == jnp.arange(slot_limit)[None, :, None]
    )
    picked = jnp.sum(jnp.where(wanted, slot_ids[:, None, :], 0), axis=2)
    present = jnp.any(wanted, axis=2)
    stored = cache_pages[:, 0]
    outgoing = jnp.take(stored, picked.reshape(-1), axis=0).reshape(
        owners, slot_limit, stored.shape[1], N
    )
    outgoing = jnp.where(present[:, :, None, None], outgoing, jnp.zeros((), stored.dtype))
    incoming = lax.all_to_all(outgoing, "replica", split_axis=0, concat_axis=0, tiled=True)
    own_holders = lax.dynamic_index_in_dim(holders, self_index, 0, keepdims=False)
    own_ranks = lax.dynamic_index_in_dim(ranks, self_index, 0, keepdims=False)
    arrived = jnp.take(
        incoming.reshape(owners * slot_limit, stored.shape[1], N),
        own_holders * slot_limit + own_ranks,
        axis=0,
    )
    carried_state = arrived.reshape(req_here, heads_here, P_SIZE, N).astype(jnp.float32)
    decay_rate = -jnp.exp(a_log)
    spans_x = missed_x.reshape(req_here, MISS_MAX, SPAN, heads_here, P_SIZE)
    spans_b = missed_b.reshape(req_here, MISS_MAX, SPAN, groups_here, N)
    spans_dt = missed_dt.reshape(req_here, MISS_MAX, SPAN, heads_here)
    for position in range(MISS_MAX):
        step_size = jax.nn.softplus(spans_dt[:, position] + dt_bias)
        updated = state_update(
            spans_x[:, position],
            spans_b[:, position],
            step_size,
            decay_rate * step_size,
            carried_state,
        )
        active = position >= MISS_MAX - missed
        carried_state = jnp.where(active[:, None, None, None], updated, carried_state)
    step_size = jax.nn.softplus(suffix_dt.reshape(req_here, SPAN, heads_here) + dt_bias)
    values = span_output(
        suffix_x.reshape(req_here, SPAN, heads_here, P_SIZE),
        suffix_b.reshape(req_here, SPAN, groups_here, N),
        suffix_c.reshape(req_here, SPAN, groups_here, N),
        step_size,
        decay_rate * step_size,
        carried_state,
        skip_weight_per_head,
    )
    hidden = gate_norm(values, suffix_z, norm_gain, groups_here)
    partial_out = (
        jnp.dot(
            hidden,
            lax.all_gather(out_weight, "replica", axis=1, tiled=True),
            preferred_element_type=jnp.float32,
        )
        .astype(jnp.bfloat16)
        .astype(jnp.float32)
    )
    return lax.psum_scatter(
        partial_out.astype(jnp.bfloat16), "tensor", scatter_dimension=1, tiled=True
    )


def solution(mesh):
    in_specs = (
        P("replica", "tensor"),
        P("replica", "tensor"),
        P("replica", "tensor"),
        P("replica", "tensor"),
        P("replica", "tensor"),
        P("replica", "tensor"),
        P("replica", "tensor"),
        P("replica", "tensor"),
        P("tensor"),
        P("tensor"),
        P("tensor"),
        P("tensor"),
        P("tensor", "replica"),
        P("replica", "tensor", None, None),
        P("tensor", None, None, None),
        P("tensor", None, None),
        P("replica"),
    )
    out_specs = P("replica", "tensor")
    return jax.shard_map(
        per_device, mesh=mesh, in_specs=in_specs, out_specs=out_specs, check_vma=False
    )
```

profile of v0, /device:TPU:1, one launch (start us, length us, event | category | flops | bytes accessed | tf_op | source)
XLA Modules:
  0.0 254.3 jit_solution(12392462511220944153)
XLA Ops:
  6.5 0.7 all-gather.2.cloned.1.call-update
  7.3 0.8 copy.64
  8.2 0.8 copy.66
  9.1 1.9 convert_reduce_fusion
  11.0 0.1 select_reduce_fusion
  11.2 0.1 reshape.357
  11.3 0.1 copy.67
  11.5 0.1 fusion.45
  11.6 0.1 copy.65
  11.7 0.7 gather_fusion
  12.4 1.6 select_select_fusion
  14.0 19.5 %all-to-all-start = ((bf16[64,2,32,256]{3,2,1,0:T(8,128)(2,1)}), bf16[64,2,32,256]{3,2,1,0:T(8,128)(2,1)}, u32[]{:S(2)}, u32[]{:S(2)}) async-start(bf16[64,2,32,256]{3,2,1,0:T(8,128)(2,1)} %select_select_fusion), calls=%async_computation | async-start | bytes 4194304 | tf_op jit(solution)/shard_map/all_to_all | solution.py:109
  33.5 0.2 reduce-scatter.2.cloned.1.call-start
  33.9 0.1 copy.92
  34.0 0.1 copy.93
  34.1 0.1 copy.94
  34.2 0.1 copy.54
  34.3 1.0 broadcast_multiply_fusion.3
  35.3 0.2 reduce_window_sum.22
  35.5 0.7 exp.102
  36.2 0.7 copy.55
  36.9 1.9 reshape.390
  38.8 1.6 reshape.389
  40.4 1.1 reduce_window_sum.23
  41.5 1.1 reduce_window_sum.27
  42.6 0.2 reduce_window_sum.32
  42.8 0.6 exp.94
  43.4 0.5 exp.96
  43.9 0.6 exp.98
  44.5 1.0 exponential_multiply_fusion.2
  45.5 1.6 copy.69
  47.1 4.2 %reshape.359 = bf16[2,3,128,16,64]{2,1,0,4,3:T(4,128)(2,1)S(1)} reshape(bf16[768,1024]{0,1:T(8,128)(2,1)} %copy.69) | data formatting | bytes 3145728 | tf_op jit(solution)/shard_map/reshape | solution.py:119
  51.4 0.7 copy.73
  52.1 0.7 copy.76
  52.7 0.5 broadcast.248
  53.3 1.8 fusion.51
  55.2 0.1 broadcast_in_dim.117
  55.3 0.7 broadcast_in_dim.118
  56.0 0.7 copy.79
  56.7 1.6 copy.57
  58.3 3.3 %copy.81 = f32[2,128,1,16,64]{1,4,3,0,2:T(8,128)} copy(f32[2,128,1,16,64]{4,3,1,0,2:T(8,128)} %reshape.390) | data formatting | bytes 2097152 | tf_op jit(solution)/shard_map/convert_element_type | solution.py:52
  61.6 0.2 convolution_bitcast_fusion.1
  61.8 0.8 copy.58
  62.6 1.2 copy.83
  63.8 0.6 fusion.47
  64.4 0.6 pad_clamp_fusion
  65.0 0.6 iota_compare_fusion.1
  65.6 1.3 broadcast_compare_fusion.3
  66.9 2.9 %slice_convert_fusion.2 = (f32[2,1,128,16,64]{2,1,0,4,3:T(1,128)S(1)}, f32[2,1,128,16,64]{2,1,0,4,3:T(1,128)S(1)}, f32[2,1,128,16,64]{2,1,0,4,3:T(1,128)S(1)}) fusion(bf16[2,3,128,16,64]{2,1,0,4,3:T(4,128)(2,1)S(1)} %reshape.359), kind=kLoop, calls=%fused_computation.30 | loop fusion | flops 786432 | bytes 4718592 | tf_op jit(solution)/shard_map/convert_element_type | solution.py:18
  69.8 0.5 multiply_convert_fusion.5
  70.3 0.5 multiply_convert_fusion.4
  70.8 0.5 multiply_convert_fusion.3
  71.3 0.4 fusion.39
  71.7 1.7 fusion.37
  73.4 1.7 fusion.35
  75.2 64.5 %all-to-all-done = bf16[64,2,32,256]{3,2,1,0:T(8,128)(2,1)} async-done(((bf16[64,2,32,256]{3,2,1,0:T(8,128)(2,1)}), bf16[64,2,32,256]{3,2,1,0:T(8,128)(2,1)}, u32[]{:S(2)}, u32[]{:S(2)}) %all-to-all-start) | async-done | bytes 2097184 | tf_op jit(solution)/shard_map/all_to_all | solution.py:109
  139.7 3.3 %gather_fusion.1 = bf16[64,32,256]{2,1,0:T(8,128)(2,1)} fusion(bf16[128,32,256]{2,1,0:T(8,128)(2,1)} %bitcast.18, s32[1024]{0:T(1024)} %pad_clamp_fusion), kind=kCustom, calls=%fused_computation.1 | custom fusion | bytes 2097408 | tf_op jit(solution)/shard_map/jit(_take)/gather | solution.py:112
  143.0 4.3 %fusion.13 = f32[2,128,1,16,64]{1,4,3,0,2:T(8,128)S(1)} fusion(bf16[2,128,256,1]{2,1,3,0:T(8,128)(2,1)S(1)} %bitcast.129, f32[2,16,64,256]{3,2,1,0:T(8,128)} %fusion.35, f32[2,16,64,256]{3,2,1,0:T(8,128)} %fusion.37, f32[2,16,64,256]{3,2,1,0:T(8,128)S(1)} %fusion.39, bf16[2,16,64,256]{3,2,1,0:T(8,128)(2,1)} %bitcast.122, f32[2,16]{1,0:T(2,128)} %exp.98, ...), kind=kOutput, calls=%fused_computation.22 | convolution fusion | flops 811335680 | bytes 8538502 | tf_op jit(solution)/shard_map/rlgn,rgkpn->rlgkp/dot_general | solution.py:45
  147.4 1.2 fusion.12
  148.6 0.8 copy.82
  149.4 0.4 multiply_reduce_fusion
  149.8 48.1 %all-gather.2.cloned.1.call-done = bf16[1024,4096]{0,1:T(8,128)(2,1)} async-done(((bf16[1024,64]{0,1:T(8,128)(2,1)}), bf16[1024,4096]{0,1:T(8,128)(2,1)}) %all-gather.2.cloned.1.call-update) | async-done | bytes 8388624 | tf_op jit(solution)/shard_map/all_gather | solution.py:147
  197.9 7.4 %convolution_convert_fusion = bf16[256,4096]{1,0:T(8,128)(2,1)} fusion(bf16[1024,4096]{0,1:T(8,128)(2,1)} %all-gather.2.cloned.1.call-done, f32[1024]{0:T(1024)S(1)} %copy-done.22, f32[256]{0:T(256)S(1)} %add_rsqrt_fusion, bf16[256,1024]{0,1:T(8,128)(2,1)S(1)} %copy.83, f32[128,8,2,128]{3,2,1,0:T(2,128)S(1)} %bitcast.124), kind=kOutput, calls=%fused_computation.2 | convolution fusion | flops 2150891520 | bytes 12063744 | tf_op jit(solution)/shard_map/dot_general | solution.py:145
  205.4 42.1 %reduce-scatter.2.cloned.1.call-done = bf16[256,512]{1,0:T(8,128)(2,1)} async-done(((bf16[256,4096]{1,0:T(8,128)(2,1)}), bf16[256,512]{1,0:T(8,128)(2,1)}) %reduce-scatter.2.cloned.1.call-update) | async-done | bytes 262160 | tf_op jit(solution)/shard_map/reduce_scatter | solution.py:153
  (70 shorter events, 0.7 us)
Async XLA Ops:
  6.5 5.2 %copy-start = (bf16[48,1,32,256]{3,2,1,0:T(8,128)(2,1)S(1)}, bf16[48,1,32,256]{3,2,1,0:T(8,128)(2,1)}, u32[]{:S(2)}) copy-start(bf16[48,1,32,256]{3,2,1,0:T(8,128)(2,1)} %param.30) | copy-start | bytes 2359300
  6.5 191.4 %all-gather.2.cloned.1.call-start = ((), (), s32[]{:S(2)}) async-start(), calls=%async_computation.2 | async-start | bytes 8519680 | tf_op jit(solution)/shard_map/all_gather | solution.py:147
  10.9 0.8 copy-start.10
  14.0 19.8 %copy-start.16 = (f32[768,16]{0,1:T(8,128)S(1)}, f32[768,16]{0,1:T(8,128)}, u32[]{:S(2)}) copy-start(f32[768,16]{0,1:T(8,128)} %param.24) | copy-start | bytes 147460
  14.0 20.2 %copy-start.17 = (f32[256,16]{0,1:T(8,128)S(1)}, f32[256,16]{0,1:T(8,128)}, u32[]{:S(2)}) copy-start(f32[256,16]{0,1:T(8,128)} %param.21) | copy-start | bytes 49156
  14.0 20.3 %copy-start.23 = (f32[16]{0:T(128)S(1)}, f32[16]{0:T(128)}, u32[]{:S(2)}) copy-start(f32[16]{0:T(128)} %param.26) | copy-start | bytes 196
  14.0 20.3 %copy-start.21 = (f32[16]{0:T(128)S(1)}, f32[16]{0:T(128)}, u32[]{:S(2)}) copy-start(f32[16]{0:T(128)} %param.25) | copy-start | bytes 196
  14.0 125.7 %all-to-all-start = ((bf16[64,2,32,256]{3,2,1,0:T(8,128)(2,1)}), bf16[64,2,32,256]{3,2,1,0:T(8,128)(2,1)}, u32[]{:S(2)}, u32[]{:S(2)}) async-start(bf16[64,2,32,256]{3,2,1,0:T(8,128)(2,1)} %select_select_fusion), calls=%async_computation | async-start | bytes 4194304 | tf_op jit(solution)/shard_map/all_to_all | solution.py:109
  33.5 3.3 %copy-start.1 = (bf16[256,1024]{1,0:T(8,128)(2,1)S(1)}, bf16[256,1024]{1,0:T(8,128)(2,1)}, u32[]{:S(2)}) copy-start(bf16[256,1024]{1,0:T(8,128)(2,1)} %param.17) | copy-start | bytes 1572868
  33.5 213.9 %reduce-scatter.2.cloned.1.call-start = ((), (), s32[]{:S(2)}) async-start(), calls=%async_computation.3 | async-start | bytes 2359296 | tf_op jit(solution)/shard_map/reduce_scatter | solution.py:153
  38.8 6.8 %copy-start.2 = (bf16[768,1024]{1,0:T(8,128)(2,1)S(1)}, bf16[768,1024]{1,0:T(8,128)(2,1)}, u32[]{:S(2)}) copy-start(bf16[768,1024]{1,0:T(8,128)(2,1)} %param.22) | copy-start | bytes 4718596
  47.1 4.2 %copy-start.7 = (f32[2,128,16]{2,1,0:T(8,128)S(1)}, f32[2,128,16]{2,1,0:T(8,128)}, u32[]{:S(2)}) copy-start(f32[2,128,16]{2,1,0:T(8,128)} %get-tuple-element.22) | copy-start | bytes 49156
  47.1 4.9 %copy-start.6 = (f32[2,128,16]{2,1,0:T(8,128)S(1)}, f32[2,128,16]{2,1,0:T(8,128)}, u32[]{:S(2)}) copy-start(f32[2,128,16]{2,1,0:T(8,128)} %get-tuple-element.23) | copy-start | bytes 49156
  47.1 8.9 %copy-start.8 = (f32[2,128,16]{2,1,0:T(8,128)S(1)}, f32[2,128,16]{2,1,0:T(8,128)}, u32[]{:S(2)}) copy-start(f32[2,128,16]{2,1,0:T(8,128)} %exp.102) | copy-start | bytes 49156
  51.4 10.2 %copy-start.5 = (bf16[256,256]{1,0:T(8,128)(2,1)S(1)}, bf16[256,256]{1,0:T(8,128)(2,1)}, u32[]{:S(2)}) copy-start(bf16[256,256]{1,0:T(8,128)(2,1)} %param.20) | copy-start | bytes 393220
  52.1 9.6 %copy-start.11 = (bf16[256,256]{1,0:T(8,128)(2,1)S(1)}, bf16[256,256]{1,0:T(8,128)(2,1)}, u32[]{:S(2)}) copy-start(bf16[256,256]{1,0:T(8,128)(2,1)} %param.19) | copy-start | bytes 393220
  66.9 3.4 %copy-start.14 = (f32[2,128,16]{1,0,2:T(2,128)S(1)}, f32[2,128,16]{1,0,2:T(2,128)}, u32[]{:S(2)}) copy-start(f32[2,128,16]{1,0,2:T(2,128)} %copy.73) | copy-start | bytes 49156
  69.7 1.0 copy-start.13
  69.8 1.5 copy-start.9
  73.4 69.6 %copy-start.15 = (f32[2,128,16]{1,2,0:T(8,128)S(1)}, f32[2,128,16]{1,2,0:T(8,128)}, u32[]{:S(2)}) copy-start(f32[2,128,16]{1,2,0:T(8,128)} %copy.79) | copy-start | bytes 49156
  143.0 4.3 %copy-start.3 = (f32[2,128,1,16,64]{1,4,3,0,2:T(8,128)S(1)}, f32[2,128,1,16,64]{1,4,3,0,2:T(8,128)}, u32[]{:S(2)}) copy-start(f32[2,128,1,16,64]{1,4,3,0,2:T(8,128)} %copy.81) | copy-start | bytes 3145732
  143.0 4.3 %copy-start.4 = (bf16[2,128,16,64]{3,2,1,0:T(8,128)(2,1)S(1)}, bf16[2,128,16,64]{3,2,1,0:T(8,128)(2,1)}, u32[]{:S(2)}) copy-start(bf16[2,128,16,64]{3,2,1,0:T(8,128)(2,1)} %reshape.389) | copy-start | bytes 1572868
  143.0 4.3 %copy-start.12 = (f32[2,128,128]{2,1,0:T(8,128)S(1)}, f32[2,128,128]{2,1,0:T(8,128)}, u32[]{:S(2)}) copy-start(f32[2,128,128]{2,1,0:T(8,128)} %copy.58) | copy-start | bytes 393220
  143.0 4.3 %copy-start.18 = (f32[2,128,16]{1,2,0:T(8,128)S(1)}, f32[2,128,16]{1,2,0:T(8,128)}, u32[]{:S(2)}) copy-start(f32[2,128,16]{1,2,0:T(8,128)} %copy.55) | copy-start | bytes 49156
  143.0 4.3 %copy-start.19 = (f32[2,128,16]{1,2,0:T(8,128)S(1)}, f32[2,128,16]{1,2,0:T(8,128)}, u32[]{:S(2)}) copy-start(f32[2,128,16]{1,2,0:T(8,128)} %copy.57) | copy-start | bytes 49156
  143.0 4.3 %copy-start.20 = (pred[128,128]{1,0:T(8,128)(4,1)S(1)}, pred[128,128]{1,0:T(8,128)(4,1)}, u32[]{:S(2)}) copy-start(pred[128,128]{1,0:T(8,128)(4,1)} %iota_compare_fusion.1) | copy-start | bytes 49156
  143.0 4.3 %copy-start.24 = (f32[16]{0:T(128)S(1)}, f32[16]{0:T(128)}, u32[]{:S(2)}) copy-start(f32[16]{0:T(128)} %param.27) | copy-start | bytes 196
  148.6 49.4 %copy-start.22 = (f32[1024]{0:T(1024)S(1)}, f32[1024]{0:T(1024)}, u32[]{:S(2)}) copy-start(f32[1024]{0:T(1024)} %param.28) | copy-start | bytes 12292
Sparse Core Ops, SparseCore 0:
  10.3 187.5 all-gather.1
  205.5 41.9 reduce-scatter.1
where the time goes:
time: 256 us; the launch traced here: 254 us
  waiting for transfers between devices  155 us (61%)
  local copies, waits for them, and re-layouts  30.4 us (12%)
  starting transfers between devices  19.7 us (8%)
  other arithmetic  17.9 us (7%)
  matrix products  16.9 us (7%)
  between operations  13.8 us (5%)
    all_to_all x1, waiting for transfers between devices, per_device(): lax.all_to_all(outgoing, 'replica', split_axis=0, concat_axis=0, tiled=True)  64.5 us
    all_gather x1, waiting for transfers between devices, per_device(): lax.all_gather(out_weight, 'replica', axis=1, tiled=True)  48.1 us
    reduce_scatter x1, waiting for transfers between devices, per_device(): lax.psum_scatter(partial_out.astype(jnp.bfloat16), 'tensor', scatter_dime...  42.1 us
    all_to_all x1, starting transfers between devices, per_device(): lax.all_to_all(outgoing, 'replica', split_axis=0, concat_axis=0, tiled=True)  19.5 us
    dot_general x1, matrix products, per_device(): jnp.dot(hidden, lax.all_gather(out_weight, 'replica', axis=1, tiled=True)...  7.41 us
    convert_element_type x2, local copies, waits for them, and re-layouts, span_output(): grouped_x.astype(jnp.float32)  5.23 us
  transfers between devices with their start and end apart: 3, of which 3 were waited for; matrix products, arithmetic and copies ran while one was open for 23% of the time, Pallas kernels for 0%

commit v1 on v0

v1 whole, which is shorter than its diff:
```python
import functools

import jax
import jax.numpy as jnp
from jax import lax
from jax.experimental import pallas as pl
from jax.experimental.pallas import tpu as pltpu
from jax.sharding import PartitionSpec as P

MESH = pl.DeviceIdType.MESH
P_SIZE = 64
N = 256
SPAN = 128
MISS = 3
REQ = 2
HEADS = 16
WIDTH = HEADS * P_SIZE
X = 4
ROWS = 32
F32 = jnp.float32
BF16 = jnp.bfloat16
NT = (((1,), (1,)), ((), ()))
HIGHEST = lax.Precision.HIGHEST


def dot(a, b, precision=None):
    return jnp.dot(a, b, preferred_element_type=F32, precision=precision)


def dot_nt(a, b):
    return lax.dot_general(a, b, NT, preferred_element_type=F32)


def iota(shape, dim):
    return lax.broadcasted_iota(jnp.int32, shape, dim)


def split(v):
    high = v.astype(BF16)
    return jnp.concatenate([high, (v - high.astype(F32)).astype(BF16)], axis=1)


def kernel(
    Z, T,
    picks, reqs, places, missed, dt_ref, bias, a_log, skip, gain,
    sx, sz, sb, sc, mx, mb, w_ref, cache,
    out_ref,
    wt, cg, outp, pg, relay, sp, rp, pt, a0, a1, xs, qs, hid,
    cs, cr, ws, wr, wxs, wxr, wfs, wfr, pgs, pgr, pjs, pjr,
    xsend, xrecv, ysend, yrecv, coresem_s, coresem_r, ys_s, ys_r,
):
    H = Z // 2
    r = lax.axis_index("replica")
    t = lax.axis_index("tensor")
    x = r // Z
    z = r % Z

    def zmod(v):
        return lax.rem(v + Z, Z)

    def at(xx, zz):
        return {"replica": lax.rem(xx + X, X) * Z + zmod(zz), "tensor": t}

    right_x, left_x = at(x + 1, z), at(x - 1, z)
    up_z, down_z = at(x, z + 1), at(x, z - 1)
    peers = [at(x, z + s) for s in range(1, Z)] + [right_x, left_x]
    if T > 1:
        y, c = t // 2, t % 2
        Y = T // 2
        other = {"replica": r, "tensor": y * 2 + 1 - c}
        y_up = {"replica": r, "tensor": lax.rem(y + 1, Y) * 2 + c}
        y_down = {"replica": r, "tensor": lax.rem(y + Y - 1, Y) * 2 + c}
        peers += [other, y_up, y_down]

    barrier = pltpu.get_barrier_semaphore()
    for peer in peers:
        pl.semaphore_signal(barrier, inc=1, device_id=peer, device_id_type=MESH)

    def w_rows(xx, zz, lo=0, count=64):
        start = (lax.rem(xx + X, X) * Z + zmod(zz)) * 64 + lo
        return wt.at[pl.ds(pl.multiple_of(start, 16), count)]

    eye64 = (iota((64, 64), 0) == iota((64, 64), 1)).astype(BF16)
    wt[pl.ds(pl.multiple_of(r * 64, 16), 64), :] = dot_nt(eye64, w_ref[...]).astype(BF16)
    cg[z] = sc[...]

    def fetch(k, carry):
        for g in range(4):
            for s in range(2):
                page = cache[picks[(g * Z + k) * 2 + s]]
                if g == 0:
                    pg[0, k, s * ROWS:(s + 1) * ROWS, :] = page
                else:
                    outp[g - 1, k, s * ROWS:(s + 1) * ROWS, :] = page
        return carry

    lax.fori_loop(0, Z, fetch, 0)
    pl.semaphore_wait(barrier, len(peers))

    sends = []

    def send(src, dst, ssem, rsem, device):
        copy = pltpu.make_async_remote_copy(
            src_ref=src, dst_ref=dst, send_sem=ssem, recv_sem=rsem,
            device_id=device, device_id_type=MESH,
        )
        copy.start()
        sends.append(copy)

    def arrived(ref, ssem, rsem, device):
        pltpu.make_async_remote_copy(
            src_ref=ref, dst_ref=ref, send_sem=ssem, recv_sem=rsem,
            device_id=device, device_id_type=MESH,
        ).wait_recv()

    def c_part(d, step):
        block = zmod(z - step) if d == 0 else zmod(z + step)
        if step < H:
            return cg.at[block]
        return cg.at[block, pl.ds(d * SPAN, SPAN)]

    def c_send(d, step):
        block = zmod(z - step + 1) if d == 0 else zmod(z + step - 1)
        part = cg.at[block] if step < H else cg.at[block, pl.ds(d * SPAN, SPAN)]
        send(part, part, cs.at[d, step - 1], cr.at[d, step - 1], (up_z, down_z)[d])

    def w_part(d, step):
        zz = z - step if d == 0 else z + step
        return w_rows(x, zz) if step < H else w_rows(x, zz, d * 32, 32)

    def w_send(d, step):
        zz = z - step + 1 if d == 0 else z + step - 1
        part = w_rows(x, zz) if step < H else w_rows(x, zz, d * 32, 32)
        send(part, part, ws.at[d, step - 1], wr.at[d, step - 1], (up_z, down_z)[d])

    def z_of(k):
        if k == 0:
            return z
        step = (k + 1) // 2
        return z - step if k % 2 == 1 else z + step

    def wx_send(k):
        part = w_rows(x, z_of(k))
        send(part, part, wxs.at[0, k], wxr.at[0, k], right_x)
        send(part, part, wxs.at[1, k], wxr.at[1, k], left_x)

    def wx_pass(k):
        arrived(w_rows(x - 1, z_of(k)), wxs.at[0, k], wxr.at[0, k], right_x)
        part = w_rows(x - 1, z_of(k), 0, 32)
        send(part, part, wfs.at[0, k], wfr.at[0, k], right_x)
        arrived(w_rows(x + 1, z_of(k)), wxs.at[1, k], wxr.at[1, k], left_x)
        part = w_rows(x + 1, z_of(k), 32, 32)
        send(part, part, wfs.at[1, k], wfr.at[1, k], left_x)

    send(outp.at[2, pl.ds(0, H)], relay.at[0], pgs.at[0], pgr.at[0], right_x)
    send(outp.at[2, pl.ds(H, H)], relay.at[1], pgs.at[1], pgr.at[1], left_x)
    c_send(0, 1)
    c_send(1, 1)
    send(outp.at[0], pg.at[1], pgs.at[2], pgr.at[2], right_x)
    send(outp.at[1], pg.at[2], pgs.at[3], pgr.at[3], left_x)
    w_send(0, 1)
    w_send(1, 1)

    def pages_pass():
        arrived(relay.at[0], pgs.at[0], pgr.at[0], right_x)
        send(relay.at[0], pg.at[3, pl.ds(0, H)], pgs.at[4], pgr.at[4], right_x)
        arrived(relay.at[1], pgs.at[1], pgr.at[1], left_x)
        send(relay.at[1], pg.at[3, pl.ds(H, H)], pgs.at[5], pgr.at[5], left_x)

    def pages_wait():
        arrived(pg.at[1], pgs.at[2], pgr.at[2], right_x)
        arrived(pg.at[2], pgs.at[3], pgr.at[3], left_x)
        arrived(pg.at[3, pl.ds(0, H)], pgs.at[4], pgr.at[4], right_x)
        arrived(pg.at[3, pl.ds(H, H)], pgs.at[5], pgr.at[5], left_x)

    def project(dz):
        pages = jnp.concatenate([pg[g, dz] for g in range(4)], axis=0)
        full = dot_nt(pages, cg[dz])
        parts = []
        for k in range(8):
            second = reqs[dz * 8 + k]
            rows = full[k * ROWS:(k + 1) * ROWS]
            parts.append(rows[:, :SPAN] * (1.0 - second) + rows[:, SPAN:] * second)
        return jnp.stack(parts).astype(BF16)

    def rp_of(zz):
        return rp.at[pl.ds(zz * 2 * X, 2 * X)]

    def project_send(dz, sem):
        sp[sem] = project(dz)
        send(sp.at[sem], rp_of(z), pjs.at[sem], pjr.at[sem], at(x, dz))

    def project_step(step):
        if step == 0:
            rp[pl.ds(z * 2 * X, 2 * X)] = project(z)
            return
        project_send(zmod(z + step), 2 * step - 2)
        if step < H:
            project_send(zmod(z - step), 2 * step - 1)

    lane = iota((1, SPAN), 1)
    lane_block = (lane // HEADS) % 4

    def decays():
        rows, cols = iota((SPAN, SPAN), 0), iota((SPAN, SPAN), 1)
        first = lane < 64
        count = jnp.where(first, missed[0], missed[1])
        active = jnp.where(lane_block == 3, 1, (lane_block >= MISS - count).astype(jnp.int32))
        active = active.astype(F32)
        raw = dt_ref[...] + bias[...]
        dt = jnp.maximum(raw, 0.0) + jnp.log1p(jnp.exp(-jnp.abs(raw)))
        dt = dt * active
        q = dot((rows >= cols).astype(F32), -jnp.exp(a_log[...]) * dt, HIGHEST)
        row_block, col_block = (rows // HEADS) % 4, (cols // HEADS) % 4
        later = (row_block < 3) & ((row_block >= col_block) | (col_block == 3))
        same = (rows // 64 == cols // 64) & (rows % HEADS == cols % HEADS)
        last = jnp.broadcast_to(q[SPAN - 1:, :], (8, SPAN))
        tail = dot(last, (later & same).astype(F32), HIGHEST)[0:1]
        weight = jnp.exp(jnp.where(lane_block == 3, q, tail - q))
        weight = jnp.where(lane_block == 3, weight, weight * dt)
        qs[0] = q
        qs[1] = q.T
        qs[2] = dt.T
        qs[3] = weight
        qs[4] = jnp.exp(jnp.where(lane_block == 3, q + tail, 0.0))

    def spread(values, block):
        chosen = jnp.where(lane // HEADS == block, values, 0.0)
        heads = iota((2 * SPAN, WIDTH), 0) % HEADS
        picked = (heads == iota((2 * SPAN, WIDTH), 1) // P_SIZE).astype(BF16)
        return dot(split(chosen), picked)

    def missed_block(q_, b):
        weight = spread(qs[3], q_ * 4 + b)
        at_ = (q_ * MISS + b) * SPAN
        xs[b * SPAN:(b + 1) * SPAN, :] = (mx[at_:at_ + SPAN, :].astype(F32) * weight).astype(BF16)

    def carried(q_):
        rows = slice(q_ * SPAN, (q_ + 1) * SPAN)
        scores = dot_nt(sc[rows, :], mb[q_ * MISS * SPAN:(q_ + 1) * MISS * SPAN, :])
        rest = dot(scores.astype(BF16), xs[...])
        a0[rows, :] = rest * spread(qs[3], q_ * 4 + 3) + skip[...] * sx[rows, :].astype(F32)
        qs[5] = dot_nt(sc[rows, :], sb[rows, :])

    def pair(q_, p):
        rows = slice(q_ * SPAN, (q_ + 1) * SPAN)
        cols = slice(p * 2 * P_SIZE, (p + 1) * 2 * P_SIZE)
        causal = iota((SPAN, SPAN), 0) >= iota((SPAN, SPAN), 1)
        mixes = []
        for h in range(2):
            at_ = q_ * 64 + 48 + p * 2 + h
            gap = jnp.where(causal, qs[0, :, at_:at_ + 1] - qs[1, at_:at_ + 1, :], -jnp.inf)
            mixes.append((jnp.exp(gap) * qs[2, at_:at_ + 1, :] * qs[5]).astype(BF16))
        two = sx[rows, cols]
        low = iota((SPAN, 2 * P_SIZE), 1) < P_SIZE
        zero = jnp.zeros_like(two)
        stacked = jnp.concatenate([jnp.where(low, two, zero), jnp.where(low, zero, two)], axis=0)
        a0[rows, cols] += dot(jnp.concatenate(mixes, axis=1), stacked)

    def gates(q_):
        rows = slice(q_ * SPAN, (q_ + 1) * SPAN)
        v = sz[rows, :].astype(F32)
        gate = v / (1.0 + jnp.exp(-v))
        a0[rows, :] = a0[rows, :] * gate
        a1[rows, :] = spread(qs[4], q_ * 4 + 3) * gate

    work = [decays]
    for q_ in range(REQ):
        work += [functools.partial(missed_block, q_, b) for b in range(MISS)]
        work.append(functools.partial(carried, q_))
        work += [functools.partial(pair, q_, p) for p in range(HEADS // 2)]
        work.append(functools.partial(gates, q_))

    LAG = min(3, H)
    steps = H + LAG + 1
    share = -(-len(work) // steps)
    wx_send(0)
    for i in range(1, steps + 1):
        if i <= H:
            for d in range(2):
                arrived(c_part(d, i), cs.at[d, i - 1], cr.at[d, i - 1], (up_z, down_z)[d])
                if i < H:
                    c_send(d, i + 1)
            for d in range(2):
                arrived(w_part(d, i), ws.at[d, i - 1], wr.at[d, i - 1], (up_z, down_z)[d])
                if i < H:
                    w_send(d, i + 1)
            if i < H:
                wx_send(2 * i - 1)
                wx_send(2 * i)
            else:
                wx_send(2 * H - 1)
        if i == 2 or H == 1:
            pages_pass()
        if i == LAG + 1:
            pages_wait()
        if i > LAG:
            if i == LAG + 1:
                project_step(0)
            if i - LAG <= H:
                project_step(i - LAG)
        for _ in range(share):
            if work:
                work.pop(0)()
        if i == 2:
            wx_pass(0)
        if 3 <= i <= H + 2:
            for k in (2 * (i - 2) - 1, 2 * (i - 2)):
                if k < Z:
                    wx_pass(k)
    while work:
        work.pop(0)()

    for step in range(1, H + 1):
        arrived(rp_of(zmod(z - step)), pjs.at[2 * step - 2], pjr.at[2 * step - 2], up_z)
        if step < H:
            arrived(rp_of(zmod(z + step)), pjs.at[2 * step - 1], pjr.at[2 * step - 1], up_z)

    eye = (iota((SPAN, SPAN), 0) == iota((SPAN, SPAN), 1)).astype(BF16)
    for q_ in range(REQ):
        def place(j, carry, q_=q_):
            pt[j] = rp[places[q_ * 2 * HEADS + j]]
            return carry

        lax.fori_loop(0, 2 * HEADS, place, 0, unroll=8)
        rows = slice(q_ * SPAN, (q_ + 1) * SPAN)
        g = a0[rows, :] + a1[rows, :] * dot_nt(eye, pt[...].reshape(WIDTH, SPAN))
        scale = lax.rsqrt(jnp.mean(g * g, axis=-1, keepdims=True) + 1e-05)
        hid[rows, :] = (g * scale * gain[...]).astype(BF16)

    for k in range(Z):
        arrived(w_rows(x + 2, z_of(k), 0, 32), wfs.at[0, k], wfr.at[0, k], right_x)
        arrived(w_rows(x + 2, z_of(k), 32, 32), wfs.at[1, k], wfr.at[1, k], left_x)

    cols = out_ref.shape[1]

    def product(block):
        weights = wt[pl.ds(pl.multiple_of(block * cols, cols), cols), :]
        return dot_nt(hid[...], weights)

    if T == 1:
        out_ref[...] = product(0).astype(BF16)
    else:
        offsets = (2, 1, Y - 1, 0)

        def block_of(k, core):
            return lax.rem(y + offsets[k], Y) * 2 + core

        for k in range(4):
            xsend[k] = product(block_of(k, 1 - c)).astype(BF16)
            send(xsend.at[k], xrecv.at[k], coresem_s.at[k], coresem_r.at[k], other)

        def both(k):
            mine = product(block_of(k, c))
            arrived(xrecv.at[k], coresem_s.at[k], coresem_r.at[k], other)
            return mine + xrecv[k].astype(F32)

        half = out_ref.shape[0] // 2
        lo, hi = pl.ds(0, half), pl.ds(half, half)
        ysend[0] = both(0).astype(BF16)
        send(ysend.at[0, lo], yrecv.at[0], ys_s.at[0], ys_r.at[0], y_up)
        send(ysend.at[0, hi], yrecv.at[1], ys_s.at[1], ys_r.at[1], y_down)
        up = both(1)
        ysend[1, hi] = up[half:].astype(BF16)
        send(ysend.at[1, hi], yrecv.at[2], ys_s.at[2], ys_r.at[2], y_up)
        down = both(2)
        ysend[2, lo] = down[:half].astype(BF16)
        send(ysend.at[2, lo], yrecv.at[3], ys_s.at[3], ys_r.at[3], y_down)
        arrived(yrecv.at[0], ys_s.at[0], ys_r.at[0], y_up)
        ysend[1, lo] = (up[:half] + yrecv[0].astype(F32)).astype(BF16)
        send(ysend.at[1, lo], yrecv.at[4], ys_s.at[4], ys_r.at[4], y_up)
        arrived(yrecv.at[1], ys_s.at[1], ys_r.at[1], y_down)
        ysend[2, hi] = (down[half:] + yrecv[1].astype(F32)).astype(BF16)
        send(ysend.at[2, hi], yrecv.at[5], ys_s.at[5], ys_r.at[5], y_down)
        own = both(3)
        for k in range(2, 6):
            arrived(yrecv.at[k], ys_s.at[k], ys_r.at[k], (y_up, y_down)[k % 2])
        low = own[:half] + yrecv[4].astype(F32) + yrecv[3].astype(F32)
        high = own[half:] + yrecv[2].astype(F32) + yrecv[5].astype(F32)
        out_ref[lo, :] = low.astype(BF16)
        out_ref[hi, :] = high.astype(BF16)

    for copy in sends:
        copy.wait_send()


def per_device(
    suffix_x, suffix_z, suffix_b, suffix_c, suffix_dt, missed_x, missed_b, missed_dt,
    dt_bias, a_log, skip_weight_per_head, norm_gain, out_weight, cache_pages,
    hit_holder, hit_slot, missed,
):
    R = lax.axis_size("replica")
    T = lax.axis_size("tensor")
    Z = R // X
    H = Z // 2
    r = lax.axis_index("replica")
    x, z = r // Z, r % Z
    hits = hit_holder.shape[1] * hit_holder.shape[2] // R
    holders = hit_holder[0, :, :, 0].reshape(R, hits)
    slots = hit_slot[0].reshape(R, hits)
    keys = jnp.arange(hits, dtype=jnp.int32) * 64 + slots

    def ends(mask, values):
        first = jnp.min(jnp.where(mask, values, 1 << 20), axis=-1)
        last = jnp.max(jnp.where(mask, values, -1), axis=-1)
        none = last < 0
        return jnp.stack([jnp.where(none, 0, first), jnp.where(none, 0, last)], axis=-1)

    out_order = (x + jnp.array([0, 1, 3, 2])) % X
    picks = (ends(holders == r, keys) % 64).reshape(X, Z, 2)[out_order].reshape(-1)
    in_order = (x + jnp.array([0, 3, 1, 2])) % X
    column = lax.dynamic_slice_in_dim(holders, x * Z, Z)
    column_keys = lax.dynamic_slice_in_dim(keys, x * Z, Z)
    wanted = column[None] == (in_order * Z + z)[:, None, None]
    reqs = ends(wanted, jnp.broadcast_to(column_keys[None], wanted.shape)) // (64 * hits // REQ)
    reqs = reqs.transpose(1, 0, 2).reshape(-1).astype(F32)
    own = lax.dynamic_index_in_dim(holders, r, 0, keepdims=False)
    positions = jnp.arange(hits)
    again = jnp.any((own[None] == own[:, None]) & (positions[None] < positions[:, None]), axis=1)
    relative = (x - own // Z + X) % X
    group = jnp.where(relative >= 2, 5 - relative, relative)
    places = (own % Z) * 8 + group * 2 + again.astype(jnp.int32)

    raw = jnp.concatenate(
        [missed_dt.reshape(REQ, MISS, SPAN, HEADS), suffix_dt.reshape(REQ, 1, SPAN, HEADS)], axis=1
    ).transpose(2, 0, 1, 3).reshape(SPAN, REQ * (MISS + 1) * HEADS)
    bias = jnp.tile(dt_bias, REQ * (MISS + 1))[None]
    rates = jnp.tile(a_log, REQ * (MISS + 1))[None]
    skip = jnp.repeat(skip_weight_per_head, P_SIZE)[None]

    smem = pl.BlockSpec(memory_space=pltpu.SMEM)
    vmem = pl.BlockSpec(memory_space=pltpu.VMEM)
    tokens = REQ * SPAN
    cols = out_weight.shape[1] * R // T
    V = pltpu.VMEM
    D = pltpu.SemaphoreType.DMA
    return pl.pallas_call(
        functools.partial(kernel, Z, T),
        out_shape=jax.ShapeDtypeStruct((tokens, cols), BF16),
        in_specs=[smem] * 4 + [vmem] * 13,
        out_specs=vmem,
        scratch_shapes=[
            V((R * 64, WIDTH), BF16),
            V((Z, tokens, N), BF16),
            V((3, Z, 2 * ROWS, N), BF16),
            V((4, Z, 2 * ROWS, N), BF16),
            V((2, H, 2 * ROWS, N), BF16),
            V((Z - 1, 2 * X, ROWS, SPAN), BF16),
            V((Z * 2 * X, ROWS, SPAN), BF16),
            V((2 * HEADS, ROWS, SPAN), BF16),
            V((tokens, WIDTH), F32),
            V((tokens, WIDTH), F32),
            V((MISS * SPAN, WIDTH), BF16),
            V((6, SPAN, SPAN), F32),
            V((tokens, WIDTH), BF16),
            D((2, H)), D((2, H)), D((2, H)), D((2, H)),
            D((2, Z)), D((2, Z)), D((2, Z)), D((2, Z)),
            D((6,)), D((6,)), D((Z - 1,)), D((Z - 1,)),
            V((4, tokens, cols), BF16),
            V((4, tokens, cols), BF16),
            V((3, tokens, cols), BF16),
            V((6, tokens // 2, cols), BF16),
            D((4,)), D((4,)), D((6,)), D((6,)),
        ],
        compiler_params=pltpu.CompilerParams(
            collective_id=0, has_side_effects=True, vmem_limit_bytes=58 * 1024 * 1024
        ),
        cost_estimate=pl.CostEstimate(
            flops=4 * 10**9, bytes_accessed=8 * 10**6, transcendentals=10**6
        ),
    )(
        picks.astype(jnp.int32), reqs, places.astype(jnp.int32), missed,
        raw, bias, rates, skip, norm_gain[None],
        suffix_x, suffix_z, suffix_b, suffix_c, missed_x, missed_b, out_weight,
        cache_pages[:, 0],
    )


def solution(mesh):
    in_specs = (
        P("replica", "tensor"),
        P("replica", "tensor"),
        P("replica", "tensor"),
        P("replica", "tensor"),
        P("replica", "tensor"),
        P("replica", "tensor"),
        P("replica", "tensor"),
        P("replica", "tensor"),
        P("tensor"),
        P("tensor"),
        P("tensor"),
        P("tensor"),
        P("tensor", "replica"),
        P("replica", "tensor", None, None),
        P("tensor", None, None, None),
        P("tensor", None, None),
        P("replica"),
    )
    return jax.shard_map(
        per_device, mesh=mesh, in_specs=in_specs, out_specs=P("replica", "tensor"), check_vma=False
    )
```

time: 256 us -> 157 us (0.61)
  waiting for transfers between devices: 155 us -> 0 us
  Pallas kernels: 0 us -> 141 us
  starting transfers between devices: 19.7 us -> 0 us
  local copies, waits for them, and re-layouts: 30.4 us -> 13.1 us
  matrix products: 16.9 us -> 0 us
  other arithmetic: 17.9 us -> 2.24 us
  between operations: 13.8 us -> 0.12 us
    pallas_call x0 -> x1, Pallas kernels: none -> 141 us  [per_device(): pl.pallas_call(functools.partial(kernel, Z, T), out_shape=jax.ShapeDtypeS...]
    all_to_all x1 -> x0, waiting for transfers between devices: 64.5 us -> none  [per_device(): lax.all_to_all(outgoing, 'replica', split_axis=0, concat_axis=0, tiled=True)]
    all_gather x1 -> x0, waiting for transfers between devices: 48.1 us -> none  [per_device(): lax.all_gather(out_weight, 'replica', axis=1, tiled=True)]
    reduce_scatter x1 -> x0, waiting for transfers between devices: 42.1 us -> none  [per_device(): lax.psum_scatter(partial_out.astype(jnp.bfloat16), 'tensor', scatter_dime...]
    all_to_all x1 -> x0, starting transfers between devices: 19.5 us -> none  [per_device(): lax.all_to_all(outgoing, 'replica', split_axis=0, concat_axis=0, tiled=True)]
    dot_general x7 -> x0, matrix products: 16.9 us -> none  [the longest x1 7.41 us: per_device(): jnp.dot(hidden, lax.all_gather(out_weight, 'replica', axis=1, tiled=True)...]
    convert_element_type x2, local copies, waits for them, and re-layouts: 5.23 us -> 0.78 us  [per_device(): reqs = reqs.transpose(1, 0, 2).reshape(-1).astype(F32)]
    convert_element_type x4 -> x1, other arithmetic: 4.3 us -> 0.02 us  [per_device(): reqs = reqs.transpose(1, 0, 2).reshape(-1).astype(F32)]
  transfers between devices with their start and end apart: 3 -> 0, of which waited for: 3 -> 0; matrix products, arithmetic and copies ran while one was open for 23% -> 0% of each run, Pallas kernels for 0% -> 0%
where the time goes in v1:
time: 157 us; the launch traced here: 156 us
  Pallas kernels  141 us (90%)
  local copies, waits for them, and re-layouts  13.1 us (8%)
  other arithmetic  2.24 us (1%)
    pallas_call x1, Pallas kernels, per_device(): pl.pallas_call(functools.partial(kernel, Z, T), out_shape=jax.ShapeDtypeS...  141 us
    unnamed x6, local copies, waits for them, and re-layouts  4.14 us

profile of v1, /device:TPU:1, one launch (start us, length us, event | category | flops | bytes accessed | tf_op | source)
XLA Modules:
  0.0 156.2 jit_solution(10953680151400392259)
XLA Ops:
  0.0 0.0 copy-start
  0.0 0.7 compare_select_fusion.9
  0.8 0.7 tile.4
  1.4 0.7 broadcast_in_dim_tile.6.bias
  2.1 0.7 tile.5
  2.7 0.6 broadcast_in_dim_tile.7.a_log
  3.3 0.7 broadcast_in_dim.48
  4.1 0.7 broadcast_in_dim_reshape.3.skip
  4.7 0.7 reshape.120
  5.5 0.8 copy.41
  6.3 0.1 reshape_squeeze.9
  6.4 0.2 fusion.3
  6.6 0.6 fusion.12.places
  7.2 0.8 copy.42
  8.0 0.1 select_reduce_fusion
  8.1 0.1 reshape_squeeze.10
  8.2 0.3 fusion.1
  8.5 0.1 copy.52
  8.6 0.7 convert_element_type.12.reqs
  9.3 0.1 reduce_min.30
  9.4 0.1 reduce_min.31
  9.5 0.1 reduce_min.32
  9.6 0.1 reduce_max.30
  9.8 0.1 reduce_max.31
  9.9 0.1 reduce_max.32
  10.0 0.6 gather_fusion
  10.6 0.1 copy.46
  10.7 0.7 reshape.118.picks
  11.3 0.8 reshape.119
  12.2 0.7 copy.54.dt_ref
  12.9 0.0 copy-done
  13.0 0.8 copy.55.w_ref
  13.8 140.7 %shard_map.181 = bf16[256,512]{1,0:T(8,128)(2,1)} custom-call(s32[128]{0:T(128)} %reshape.118.picks, f32[128]{0:T(128)} %convert_element_type.12.reqs, s32[64]{0:T(128)} %fusion.12.places, s32[2]{0:T(128)} %missed.1, f32[128,128]{1,0:T(8,128)} %copy.54.dt_ref, f32[1,128]{1,0:T(1,128)} %broadcast_in_dim_tile.6.bias, f32[1,128]{1,0:T(1,128)} %broadcast_in_dim_tile.7.a_log, ...), custom_call_target="tpu_custom_call" | custom-call | flops 4000000000 | bytes 8000000 | tf_op jit(solution)/shard_map/pallas_call | solution.py:437
  154.5 1.7 %copy.57 = bf16[256,512]{1,0:T(8,128)(2,1)} copy(bf16[256,512]{1,0:T(8,128)(2,1)} %shard_map.181) | data formatting | bytes 524288
  (12 shorter events, 0.2 us)
Async XLA Ops:
  0.0 12.9 %copy-start = (bf16[1024,64]{0,1:T(8,128)(2,1)S(1)}, bf16[1024,64]{0,1:T(8,128)(2,1)}, u32[]{:S(2)}) copy-start(bf16[1024,64]{0,1:T(8,128)(2,1)} %param.31) | copy-start | bytes 393220

commit v2 on v1

--- a/solution.py
+++ b/solution.py
@@ -17,6 +17,7 @@
 WIDTH = HEADS * P_SIZE
 X = 4
 ROWS = 32
+PAGES = 32
 F32 = jnp.float32
 BF16 = jnp.bfloat16
 NT = (((1,), (1,)), ((), ()))
@@ -42,10 +43,10 @@
 
 def kernel(
     Z, T,
-    picks, reqs, places, missed, dt_ref, bias, a_log, skip, gain,
+    missed, bias, a_log, skip, holders, slots, sdt, mdt, gain,
     sx, sz, sb, sc, mx, mb, w_ref, cache,
     out_ref,
-    wt, cg, outp, pg, relay, sp, rp, pt, a0, a1, xs, qs, hid,
+    tables, places, tables_v, places_v, table_sems, wt, cg, outp, pg, relay, sp, rp, pt, a0, a1, xs, qs, skips, hid,
     cs, cr, ws, wr, wxs, wxr, wfs, wfr, pgs, pgr, pjs, pjr,
     xsend, xrecv, ysend, yrecv, coresem_s, coresem_r, ys_s, ys_r,
 ):
@@ -80,22 +81,73 @@
         start = (lax.rem(xx + X, X) * Z + zmod(zz)) * 64 + lo
         return wt.at[pl.ds(pl.multiple_of(start, 16), count)]
 
-    eye64 = (iota((64, 64), 0) == iota((64, 64), 1)).astype(BF16)
-    wt[pl.ds(pl.multiple_of(r * 64, 16), 64), :] = dot_nt(eye64, w_ref[...]).astype(BF16)
+    wt[pl.ds(pl.multiple_of(r * 64, 16), 64), :] = w_ref[...]
     cg[z] = sc[...]
 
+    requests = holders.shape[2]
+    hold = holders[...].reshape(PAGES, requests)
+    page_row, request = iota((PAGES, requests), 0), iota((PAGES, requests), 1)
+    keys = ((request % REQ) * PAGES + page_row) * 64 + slots[...]
+    even = request[0:1] % REQ == 0
+
+    def ends(holder):
+        mask = hold == holder
+        first = jnp.min(jnp.where(mask, keys, 1 << 20), axis=0, keepdims=True)
+        last = jnp.max(jnp.where(mask, keys, -1), axis=0, keepdims=True)
+        first = jnp.minimum(first, pltpu.roll(first, requests - 1, 1))
+        last = jnp.maximum(last, pltpu.roll(last, requests - 1, 1))
+        none = last < 0
+        return [jnp.where(none | ~even, 0, first), jnp.where(none | ~even, 0, last)]
+
+    table_rows = [key & 63 for key in ends(r)]
+    for offset in (0, X - 1, 1, 2):
+        holder = lax.rem(x + offset, X) * Z + z
+        table_rows += [(key >= PAGES * 64).astype(jnp.int32) for key in ends(holder)]
+    table_rows += [jnp.zeros((1, requests), jnp.int32)] * (16 - len(table_rows))
+    for k, row in enumerate(table_rows):
+        tables_v[k:k + 1, :] = row
+
+    columns = [
+        jnp.sum(jnp.where(request == r * REQ + e, hold, 0), axis=1, keepdims=True) for e in range(REQ)
+    ]
+    same = page_row == request
+    as_rows = [
+        jnp.sum(jnp.where(same, jnp.broadcast_to(v, same.shape), 0), axis=0, keepdims=True)
+        for v in columns
+    ]
+    inside, earlier = request < PAGES, request < page_row
+
+    def seen(column, row, mask):
+        return jnp.max(jnp.where((column == row) & mask, 1, 0), axis=1, keepdims=True)
+
+    again = [
+        seen(columns[0], as_rows[0], earlier),
+        jnp.maximum(seen(columns[1], as_rows[0], inside), seen(columns[1], as_rows[1], earlier)),
+    ]
+    place_table = jnp.zeros((PAGES, requests), jnp.int32)
+    for e in range(REQ):
+        relative = lax.rem(x + X - columns[e] // Z, X)
+        group = jnp.where(relative >= 2, 5 - relative, relative)
+        value = (columns[e] % Z) * (2 * X) + group * 2 + again[e]
+        place_table = jnp.where(request == e, jnp.broadcast_to(value, same.shape), place_table)
+    places_v[...] = place_table
+    to_scalars = [
+        pltpu.make_async_copy(tables_v, tables, table_sems.at[0]),
+        pltpu.make_async_copy(places_v, places, table_sems.at[1]),
+    ]
+    for copy in to_scalars:
+        copy.start()
+
     def fetch(k, carry):
-        for g in range(4):
+        for g, offset in enumerate((0, 1, X - 1, 2)):
             for s in range(2):
-                page = cache[picks[(g * Z + k) * 2 + s]]
+                page = cache[tables[s, (lax.rem(x + offset, X) * Z + k) * REQ], 0]
                 if g == 0:
                     pg[0, k, s * ROWS:(s + 1) * ROWS, :] = page
                 else:
                     outp[g - 1, k, s * ROWS:(s + 1) * ROWS, :] = page
         return carry
 
-    lax.fori_loop(0, Z, fetch, 0)
-    pl.semaphore_wait(barrier, len(peers))
 
     sends = []
 
@@ -152,10 +204,14 @@
         part = w_rows(x + 1, z_of(k), 32, 32)
         send(part, part, wfs.at[1, k], wfr.at[1, k], left_x)
 
+    pl.semaphore_wait(barrier, len(peers))
+    c_send(0, 1)
+    c_send(1, 1)
+    for copy in to_scalars:
+        copy.wait()
+    lax.fori_loop(0, Z, fetch, 0)
     send(outp.at[2, pl.ds(0, H)], relay.at[0], pgs.at[0], pgr.at[0], right_x)
     send(outp.at[2, pl.ds(H, H)], relay.at[1], pgs.at[1], pgr.at[1], left_x)
-    c_send(0, 1)
-    c_send(1, 1)
     send(outp.at[0], pg.at[1], pgs.at[2], pgr.at[2], right_x)
     send(outp.at[1], pg.at[2], pgs.at[3], pgr.at[3], left_x)
     w_send(0, 1)
@@ -178,7 +234,7 @@
         full = dot_nt(pages, cg[dz])
         parts = []
         for k in range(8):
-            second = reqs[dz * 8 + k]
+            second = tables[2 + k, (x * Z + dz) * REQ].astype(F32)
             rows = full[k * ROWS:(k + 1) * ROWS]
             parts.append(rows[:, :SPAN] * (1.0 - second) + rows[:, SPAN:] * second)
         return jnp.stack(parts).astype(BF16)
@@ -201,16 +257,26 @@
     lane = iota((1, SPAN), 1)
     lane_block = (lane // HEADS) % 4
 
+    def per_head(scalars):
+        row = jnp.zeros((1, SPAN), F32)
+        for h in range(HEADS):
+            row = jnp.where(lane % HEADS == h, scalars[h], row)
+        return row
+
     def decays():
         rows, cols = iota((SPAN, SPAN), 0), iota((SPAN, SPAN), 1)
         first = lane < 64
         count = jnp.where(first, missed[0], missed[1])
         active = jnp.where(lane_block == 3, 1, (lane_block >= MISS - count).astype(jnp.int32))
         active = active.astype(F32)
-        raw = dt_ref[...] + bias[...]
+        steps = []
+        for q_ in range(REQ):
+            steps += [mdt[:, (q_ * MISS + b) * SPAN:(q_ * MISS + b + 1) * SPAN] for b in range(MISS)]
+            steps.append(sdt[:, q_ * SPAN:(q_ + 1) * SPAN])
+        raw = jnp.concatenate(steps, axis=0).T + per_head(bias)
         dt = jnp.maximum(raw, 0.0) + jnp.log1p(jnp.exp(-jnp.abs(raw)))
         dt = dt * active
-        q = dot((rows >= cols).astype(F32), -jnp.exp(a_log[...]) * dt, HIGHEST)
+        q = dot((rows >= cols).astype(F32), -jnp.exp(per_head(a_log)) * dt, HIGHEST)
         row_block, col_block = (rows // HEADS) % 4, (cols // HEADS) % 4
         later = (row_block < 3) & ((row_block >= col_block) | (col_block == 3))
         same = (rows // 64 == cols // 64) & (rows % HEADS == cols % HEADS)
@@ -223,6 +289,7 @@
         qs[2] = dt.T
         qs[3] = weight
         qs[4] = jnp.exp(jnp.where(lane_block == 3, q + tail, 0.0))
+        skips[...] = spread(jnp.broadcast_to(per_head(skip), (8, SPAN)), 0)
 
     def spread(values, block):
         chosen = jnp.where(lane // HEADS == block, values, 0.0)
@@ -239,7 +306,7 @@
         rows = slice(q_ * SPAN, (q_ + 1) * SPAN)
         scores = dot_nt(sc[rows, :], mb[q_ * MISS * SPAN:(q_ + 1) * MISS * SPAN, :])
         rest = dot(scores.astype(BF16), xs[...])
-        a0[rows, :] = rest * spread(qs[3], q_ * 4 + 3) + skip[...] * sx[rows, :].astype(F32)
+        a0[rows, :] = rest * spread(qs[3], q_ * 4 + 3) + skips[0:1, :] * sx[rows, :].astype(F32)
         qs[5] = dot_nt(sc[rows, :], sb[rows, :])
 
     def pair(q_, p):
@@ -319,7 +386,7 @@
     eye = (iota((SPAN, SPAN), 0) == iota((SPAN, SPAN), 1)).astype(BF16)
     for q_ in range(REQ):
         def place(j, carry, q_=q_):
-            pt[j] = rp[places[q_ * 2 * HEADS + j]]
+            pt[j] = rp[places[j, q_]]
             return carry
 
         lax.fori_loop(0, 2 * HEADS, place, 0, unroll=8)
@@ -393,41 +460,6 @@
     T = lax.axis_size("tensor")
     Z = R // X
     H = Z // 2
-    r = lax.axis_index("replica")
-    x, z = r // Z, r % Z
-    hits = hit_holder.shape[1] * hit_holder.shape[2] // R
-    holders = hit_holder[0, :, :, 0].reshape(R, hits)
-    slots = hit_slot[0].reshape(R, hits)
-    keys = jnp.arange(hits, dtype=jnp.int32) * 64 + slots
-
-    def ends(mask, values):
-        first = jnp.min(jnp.where(mask, values, 1 << 20), axis=-1)
-        last = jnp.max(jnp.where(mask, values, -1), axis=-1)
-        none = last < 0
-        return jnp.stack([jnp.where(none, 0, first), jnp.where(none, 0, last)], axis=-1)
-
-    out_order = (x + jnp.array([0, 1, 3, 2])) % X
-    picks = (ends(holders == r, keys) % 64).reshape(X, Z, 2)[out_order].reshape(-1)
-    in_order = (x + jnp.array([0, 3, 1, 2])) % X
-    column = lax.dynamic_slice_in_dim(holders, x * Z, Z)
-    column_keys = lax.dynamic_slice_in_dim(keys, x * Z, Z)
-    wanted = column[None] == (in_order * Z + z)[:, None, None]
-    reqs = ends(wanted, jnp.broadcast_to(column_keys[None], wanted.shape)) // (64 * hits // REQ)
-    reqs = reqs.transpose(1, 0, 2).reshape(-1).astype(F32)
-    own = lax.dynamic_index_in_dim(holders, r, 0, keepdims=False)
-    positions = jnp.arange(hits)
-    again = jnp.any((own[None] == own[:, None]) & (positions[None] < positions[:, None]), axis=1)
-    relative = (x - own // Z + X) % X
-    group = jnp.where(relative >= 2, 5 - relative, relative)
-    places = (own % Z) * 8 + group * 2 + again.astype(jnp.int32)
-
-    raw = jnp.concatenate(
-        [missed_dt.reshape(REQ, MISS, SPAN, HEADS), suffix_dt.reshape(REQ, 1, SPAN, HEADS)], axis=1
-    ).transpose(2, 0, 1, 3).reshape(SPAN, REQ * (MISS + 1) * HEADS)
-    bias = jnp.tile(dt_bias, REQ * (MISS + 1))[None]
-    rates = jnp.tile(a_log, REQ * (MISS + 1))[None]
-    skip = jnp.repeat(skip_weight_per_head, P_SIZE)[None]
-
     smem = pl.BlockSpec(memory_space=pltpu.SMEM)
     vmem = pl.BlockSpec(memory_space=pltpu.VMEM)
     tokens = REQ * SPAN
@@ -440,6 +472,11 @@
         in_specs=[smem] * 4 + [vmem] * 13,
         out_specs=vmem,
         scratch_shapes=[
+            pltpu.SMEM((16, 2 * R), jnp.int32),
+            pltpu.SMEM((PAGES, 2 * R), jnp.int32),
+            V((16, 2 * R), jnp.int32),
+            V((PAGES, 2 * R), jnp.int32),
+            D((2,)),
             V((R * 64, WIDTH), BF16),
             V((Z, tokens, N), BF16),
             V((3, Z, 2 * ROWS, N), BF16),
@@ -452,6 +489,7 @@
             V((tokens, WIDTH), F32),
             V((MISS * SPAN, WIDTH), BF16),
             V((6, SPAN, SPAN), F32),
+            V((8, WIDTH), F32),
             V((tokens, WIDTH), BF16),
             D((2, H)), D((2, H)), D((2, H)), D((2, H)),
             D((2, Z)), D((2, Z)), D((2, Z)), D((2, Z)),
@@ -469,10 +507,9 @@
             flops=4 * 10**9, bytes_accessed=8 * 10**6, transcendentals=10**6
         ),
     )(
-        picks.astype(jnp.int32), reqs, places.astype(jnp.int32), missed,
-        raw, bias, rates, skip, norm_gain[None],
-        suffix_x, suffix_z, suffix_b, suffix_c, missed_x, missed_b, out_weight,
-        cache_pages[:, 0],
+        missed, dt_bias, a_log, skip_weight_per_head,
+        hit_holder[0].transpose(1, 2, 0), hit_slot[0].T, suffix_dt.T, missed_dt.T, norm_gain[None],
+        suffix_x, suffix_z, suffix_b, suffix_c, missed_x, missed_b, out_weight.T, cache_pages,
     )
 
 

time: 157 us -> 143 us (0.911)
  local copies, waits for them, and re-layouts: 13.1 us -> 1.67 us
  other arithmetic: 2.24 us -> 0 us
    another operation x7 -> x0, local copies, waits for them, and re-layouts: 3.4 us -> none  [the longest x2 1.32 us: per_device(): bias = jnp.tile(dt_bias, REQ * (MISS + 1))[None]]
    reshape x4 -> x0, local copies, waits for them, and re-layouts: 2.93 us -> none  [the longest x1 0.82 us: per_device(): missed_dt.reshape(REQ, MISS, SPAN, HEADS)]
    unnamed x6 -> x1, local copies, waits for them, and re-layouts: 4.14 us -> 1.67 us
where the time goes in v2:
time: 143 us
  Pallas kernels  141 us (99%)
  local copies, waits for them, and re-layouts  1.67 us (1%)
    pallas_call x1, Pallas kernels, per_device(): pl.pallas_call(functools.partial(kernel, Z, T), out_shape=jax.ShapeDtypeS...  141 us

profile of v2, /device:TPU:1, one launch (start us, length us, event | category | flops | bytes accessed | tf_op | source)
XLA Modules:
  0.0 142.9 jit_solution(17169883056433243609)
XLA Ops:
  0.0 141.2 %shard_map.163 = bf16[256,512]{1,0:T(8,128)(2,1)} custom-call(s32[2]{0:T(128)} %missed.1, f32[16]{0:T(128)} %bias.1, f32[16]{0:T(128)} %a_log.1, f32[16]{0:T(128)} %skip.1, s32[32,1,128]{2,1,0:T(1,128)} %bitcast.12, s32[32,128]{1,0:T(8,128)} %bitcast.13, f32[16,256]{1,0:T(8,128)} %bitcast.14, f32[16,768]{1,0:T(8,128)} %bitcast.11, f32[1,1024]{1,0:T(1,128)} %bitcast.15, ...), custom_call_target="tpu_custom_call" | custom-call | flops 4000000000 | bytes 8000000 | tf_op jit(solution)/shard_map/pallas_call | solution.py:469
  141.2 1.7 %copy.19 = bf16[256,512]{1,0:T(8,128)(2,1)} copy(bf16[256,512]{1,0:T(8,128)(2,1)} %shard_map.163) | data formatting | bytes 524288

commit v3 on v2

--- a/solution.py
+++ b/solution.py
@@ -16,6 +16,7 @@
 HEADS = 16
 WIDTH = HEADS * P_SIZE
 X = 4
+NCH = 4
 ROWS = 32
 PAGES = 32
 F32 = jnp.float32
@@ -139,9 +140,10 @@
         copy.start()
 
     def fetch(k, carry):
+        zz = zmod(z + (1 - 2 * (k % 2)) * ((k + 1) // 2))
         for g, offset in enumerate((0, 1, X - 1, 2)):
             for s in range(2):
-                page = cache[tables[s, (lax.rem(x + offset, X) * Z + k) * REQ], 0]
+                page = cache[tables[s, (lax.rem(x + offset, X) * Z + zz) * REQ], 0]
                 if g == 0:
                     pg[0, k, s * ROWS:(s + 1) * ROWS, :] = page
                 else:
@@ -209,50 +211,63 @@
     c_send(1, 1)
     for copy in to_scalars:
         copy.wait()
-    lax.fori_loop(0, Z, fetch, 0)
-    send(outp.at[2, pl.ds(0, H)], relay.at[0], pgs.at[0], pgr.at[0], right_x)
-    send(outp.at[2, pl.ds(H, H)], relay.at[1], pgs.at[1], pgr.at[1], left_x)
-    send(outp.at[0], pg.at[1], pgs.at[2], pgr.at[2], right_x)
-    send(outp.at[1], pg.at[2], pgs.at[3], pgr.at[3], left_x)
-    w_send(0, 1)
-    w_send(1, 1)
-
-    def pages_pass():
-        arrived(relay.at[0], pgs.at[0], pgr.at[0], right_x)
-        send(relay.at[0], pg.at[3, pl.ds(0, H)], pgs.at[4], pgr.at[4], right_x)
-        arrived(relay.at[1], pgs.at[1], pgr.at[1], left_x)
-        send(relay.at[1], pg.at[3, pl.ds(H, H)], pgs.at[5], pgr.at[5], left_x)
-
-    def pages_wait():
-        arrived(pg.at[1], pgs.at[2], pgr.at[2], right_x)
-        arrived(pg.at[2], pgs.at[3], pgr.at[3], left_x)
-        arrived(pg.at[3, pl.ds(0, H)], pgs.at[4], pgr.at[4], right_x)
-        arrived(pg.at[3, pl.ds(H, H)], pgs.at[5], pgr.at[5], left_x)
-
-    def project(dz):
-        pages = jnp.concatenate([pg[g, dz] for g in range(4)], axis=0)
+    CHUNK = Z // NCH
+    HALF = CHUNK // 2
+    for chunk in range(NCH):
+        lax.fori_loop(chunk * CHUNK, (chunk + 1) * CHUNK, fetch, 0)
+        whole = pl.ds(chunk * CHUNK, CHUNK)
+        first, second = pl.ds(chunk * CHUNK, HALF), pl.ds(chunk * CHUNK + HALF, HALF)
+        via = pl.ds(chunk * HALF, HALF)
+        ss, rs = [pgs.at[chunk, k] for k in range(6)], [pgr.at[chunk, k] for k in range(6)]
+        send(outp.at[2, first], relay.at[0, via], ss[0], rs[0], right_x)
+        send(outp.at[2, second], relay.at[1, via], ss[1], rs[1], left_x)
+        send(outp.at[0, whole], pg.at[1, whole], ss[2], rs[2], right_x)
+        send(outp.at[1, whole], pg.at[2, whole], ss[3], rs[3], left_x)
+        if chunk == 0:
+            w_send(0, 1)
+            w_send(1, 1)
+
+    def pages_pass(chunk):
+        first, second = pl.ds(chunk * CHUNK, HALF), pl.ds(chunk * CHUNK + HALF, HALF)
+        via = pl.ds(chunk * HALF, HALF)
+        ss, rs = [pgs.at[chunk, k] for k in range(6)], [pgr.at[chunk, k] for k in range(6)]
+        arrived(relay.at[0, via], ss[0], rs[0], right_x)
+        send(relay.at[0, via], pg.at[3, first], ss[4], rs[4], right_x)
+        arrived(relay.at[1, via], ss[1], rs[1], left_x)
+        send(relay.at[1, via], pg.at[3, second], ss[5], rs[5], left_x)
+
+    def pages_wait(chunk):
+        whole = pl.ds(chunk * CHUNK, CHUNK)
+        first, second = pl.ds(chunk * CHUNK, HALF), pl.ds(chunk * CHUNK + HALF, HALF)
+        ss, rs = [pgs.at[chunk, k] for k in range(6)], [pgr.at[chunk, k] for k in range(6)]
+        arrived(pg.at[1, whole], ss[2], rs[2], right_x)
+        arrived(pg.at[2, whole], ss[3], rs[3], left_x)
+        arrived(pg.at[3, first], ss[4], rs[4], right_x)
+        arrived(pg.at[3, second], ss[5], rs[5], left_x)
+
+    def rp_of(zz):
+        return rp.at[pl.ds(zz * 2 * X, 2 * X)]
+
+    waited = set()
+
+    def project(k):
+        if k // CHUNK not in waited:
+            waited.add(k // CHUNK)
+            pages_wait(k // CHUNK)
+        dz = zmod(z_of(k))
+        pages = jnp.concatenate([pg[g, k] for g in range(4)], axis=0)
         full = dot_nt(pages, cg[dz])
         parts = []
-        for k in range(8):
-            second = tables[2 + k, (x * Z + dz) * REQ].astype(F32)
-            rows = full[k * ROWS:(k + 1) * ROWS]
+        for slot in range(8):
+            second = tables[2 + slot, (x * Z + dz) * REQ].astype(F32)
+            rows = full[slot * ROWS:(slot + 1) * ROWS]
             parts.append(rows[:, :SPAN] * (1.0 - second) + rows[:, SPAN:] * second)
-        return jnp.stack(parts).astype(BF16)
-
-    def rp_of(zz):
-        return rp.at[pl.ds(zz * 2 * X, 2 * X)]
-
-    def project_send(dz, sem):
-        sp[sem] = project(dz)
-        send(sp.at[sem], rp_of(z), pjs.at[sem], pjr.at[sem], at(x, dz))
-
-    def project_step(step):
-        if step == 0:
-            rp[pl.ds(z * 2 * X, 2 * X)] = project(z)
-            return
-        project_send(zmod(z + step), 2 * step - 2)
-        if step < H:
-            project_send(zmod(z - step), 2 * step - 1)
+        products = jnp.stack(parts).astype(BF16)
+        if k == 0:
+            rp[pl.ds(z * 2 * X, 2 * X)] = products
+        else:
+            sp[k - 1] = products
+            send(sp.at[k - 1], rp_of(z), pjs.at[k - 1], pjr.at[k - 1], at(x, dz))
 
     lane = iota((1, SPAN), 1)
     lane_block = (lane // HEADS) % 4
@@ -338,50 +353,42 @@
         work += [functools.partial(pair, q_, p) for p in range(HEADS // 2)]
         work.append(functools.partial(gates, q_))
 
-    LAG = min(3, H)
-    steps = H + LAG + 1
-    share = -(-len(work) // steps)
-    wx_send(0)
-    for i in range(1, steps + 1):
+    share = -(-len(work) // (H + 1))
+    moved = passed = 0
+    for i in range(1, H + 2):
         if i <= H:
             for d in range(2):
                 arrived(c_part(d, i), cs.at[d, i - 1], cr.at[d, i - 1], (up_z, down_z)[d])
                 if i < H:
                     c_send(d, i + 1)
+        if i <= NCH:
+            pages_pass(i - 1)
+        if i > 1:
+            for k in (2 * i - 3, 2 * i - 2):
+                if k < Z:
+                    project(k)
+        if i <= H:
             for d in range(2):
                 arrived(w_part(d, i), ws.at[d, i - 1], wr.at[d, i - 1], (up_z, down_z)[d])
                 if i < H:
                     w_send(d, i + 1)
-            if i < H:
-                wx_send(2 * i - 1)
-                wx_send(2 * i)
-            else:
-                wx_send(2 * H - 1)
-        if i == 2 or H == 1:
-            pages_pass()
-        if i == LAG + 1:
-            pages_wait()
-        if i > LAG:
-            if i == LAG + 1:
-                project_step(0)
-            if i - LAG <= H:
-                project_step(i - LAG)
+        if i >= NCH:
+            while moved < min(2 * i + 1, Z):
+                wx_send(moved)
+                moved += 1
         for _ in range(share):
             if work:
                 work.pop(0)()
-        if i == 2:
-            wx_pass(0)
-        if 3 <= i <= H + 2:
-            for k in (2 * (i - 2) - 1, 2 * (i - 2)):
-                if k < Z:
-                    wx_pass(k)
-    while work:
-        work.pop(0)()
-
-    for step in range(1, H + 1):
-        arrived(rp_of(zmod(z - step)), pjs.at[2 * step - 2], pjr.at[2 * step - 2], up_z)
-        if step < H:
-            arrived(rp_of(zmod(z + step)), pjs.at[2 * step - 1], pjr.at[2 * step - 1], up_z)
+        if i >= NCH + 2:
+            for _ in range(2):
+                wx_pass(passed)
+                passed += 1
+    while passed < Z:
+        wx_pass(passed)
+        passed += 1
+    project(0)
+    for k in range(1, Z):
+        arrived(rp_of(zmod(2 * z - z_of(k))), pjs.at[k - 1], pjr.at[k - 1], up_z)
 
     eye = (iota((SPAN, SPAN), 0) == iota((SPAN, SPAN), 1)).astype(BF16)
     for q_ in range(REQ):
@@ -493,7 +500,7 @@
             V((tokens, WIDTH), BF16),
             D((2, H)), D((2, H)), D((2, H)), D((2, H)),
             D((2, Z)), D((2, Z)), D((2, Z)), D((2, Z)),
-            D((6,)), D((6,)), D((Z - 1,)), D((Z - 1,)),
+            D((NCH, 6)), D((NCH, 6)), D((Z - 1,)), D((Z - 1,)),
             V((4, tokens, cols), BF16),
             V((4, tokens, cols), BF16),
             V((3, tokens, cols), BF16),

time: 143 us -> 140 us (0.979)
  Pallas kernels: 141 us -> 138 us
    pallas_call x1, Pallas kernels: 141 us -> 138 us  [per_device(): pl.pallas_call(functools.partial(kernel, Z, T), out_shape=jax.ShapeDtypeS...]
where the time goes in v3:
time: 140 us
  Pallas kernels  138 us (99%)
  local copies, waits for them, and re-layouts  1.67 us (1%)
    pallas_call x1, Pallas kernels, per_device(): pl.pallas_call(functools.partial(kernel, Z, T), out_shape=jax.ShapeDtypeS...  138 us

profile of v3, /device:TPU:1, one launch (start us, length us, event | category | flops | bytes accessed | tf_op | source)
XLA Modules:
  0.0 140.0 jit_solution(13944609831063131874)
XLA Ops:
  0.0 138.4 %shard_map.163 = bf16[256,512]{1,0:T(8,128)(2,1)} custom-call(s32[2]{0:T(128)} %missed.1, f32[16]{0:T(128)} %bias.1, f32[16]{0:T(128)} %a_log.1, f32[16]{0:T(128)} %skip.1, s32[32,1,128]{2,1,0:T(1,128)} %bitcast.12, s32[32,128]{1,0:T(8,128)} %bitcast.13, f32[16,256]{1,0:T(8,128)} %bitcast.14, f32[16,768]{1,0:T(8,128)} %bitcast.11, f32[1,1024]{1,0:T(1,128)} %bitcast.15, ...), custom_call_target="tpu_custom_call" | custom-call | flops 4000000000 | bytes 8000000 | tf_op jit(solution)/shard_map/pallas_call | solution.py:476
  138.4 1.7 %copy.19 = bf16[256,512]{1,0:T(8,128)(2,1)} copy(bf16[256,512]{1,0:T(8,128)(2,1)} %shard_map.163) | data formatting | bytes 524288

commit v4 on v3

--- a/solution.py
+++ b/solution.py
@@ -45,9 +45,9 @@
 def kernel(
     Z, T,
     missed, bias, a_log, skip, holders, slots, sdt, mdt, gain,
-    sx, sz, sb, sc, mx, mb, w_ref, cache,
+    sx_in, sz_in, sb_in, sc, mx_in, mb_in, w_ref, cache,
     out_ref,
-    tables, places, tables_v, places_v, table_sems, wt, cg, outp, pg, relay, sp, rp, pt, a0, a1, xs, qs, skips, hid,
+    sx, sz, sb, mx, mb, load_sems, tables, places, tables_v, places_v, table_sems, wt, cg, outp, pg, relay, sp, rp, pt, a0, a1, xs, qs, skips, hid,
     cs, cr, ws, wr, wxs, wxr, wfs, wfr, pgs, pgr, pjs, pjr,
     xsend, xrecv, ysend, yrecv, coresem_s, coresem_r, ys_s, ys_r,
 ):
@@ -74,6 +74,12 @@
         y_down = {"replica": r, "tensor": lax.rem(y + Y - 1, Y) * 2 + c}
         peers += [other, y_up, y_down]
 
+    loads = [
+        pltpu.make_async_copy(src, dst, load_sems.at[k])
+        for k, (src, dst) in enumerate(
+            ((mx_in, mx), (mb_in, mb), (sx_in, sx), (sb_in, sb), (sz_in, sz))
+        )
+    ]
     barrier = pltpu.get_barrier_semaphore()
     for peer in peers:
         pl.semaphore_signal(barrier, inc=1, device_id=peer, device_id_type=MESH)
@@ -206,9 +212,13 @@
         part = w_rows(x + 1, z_of(k), 32, 32)
         send(part, part, wfs.at[1, k], wfr.at[1, k], left_x)
 
+    for load in loads:
+        load.start()
     pl.semaphore_wait(barrier, len(peers))
     c_send(0, 1)
     c_send(1, 1)
+    w_send(0, 1)
+    w_send(1, 1)
     for copy in to_scalars:
         copy.wait()
     CHUNK = Z // NCH
@@ -223,9 +233,6 @@
         send(outp.at[2, second], relay.at[1, via], ss[1], rs[1], left_x)
         send(outp.at[0, whole], pg.at[1, whole], ss[2], rs[2], right_x)
         send(outp.at[1, whole], pg.at[2, whole], ss[3], rs[3], left_x)
-        if chunk == 0:
-            w_send(0, 1)
-            w_send(1, 1)
 
     def pages_pass(chunk):
         first, second = pl.ds(chunk * CHUNK, HALF), pl.ds(chunk * CHUNK + HALF, HALF)
@@ -279,6 +286,8 @@
         return row
 
     def decays():
+        for load in loads:
+            load.wait()
         rows, cols = iota((SPAN, SPAN), 0), iota((SPAN, SPAN), 1)
         first = lane < 64
         count = jnp.where(first, missed[0], missed[1])
@@ -353,40 +362,41 @@
         work += [functools.partial(pair, q_, p) for p in range(HEADS // 2)]
         work.append(functools.partial(gates, q_))
 
-    share = -(-len(work) // (H + 1))
-    moved = passed = 0
-    for i in range(1, H + 2):
-        if i <= H:
-            for d in range(2):
-                arrived(c_part(d, i), cs.at[d, i - 1], cr.at[d, i - 1], (up_z, down_z)[d])
-                if i < H:
-                    c_send(d, i + 1)
-        if i <= NCH:
-            pages_pass(i - 1)
-        if i > 1:
-            for k in (2 * i - 3, 2 * i - 2):
-                if k < Z:
-                    project(k)
-        if i <= H:
-            for d in range(2):
-                arrived(w_part(d, i), ws.at[d, i - 1], wr.at[d, i - 1], (up_z, down_z)[d])
-                if i < H:
-                    w_send(d, i + 1)
-        if i >= NCH:
-            while moved < min(2 * i + 1, Z):
-                wx_send(moved)
-                moved += 1
+    share = -(-len(work) // H)
+    projected, moved, passed = 1, 0, 0
+    for i in range(1, H + 1):
+        for d in range(2):
+            arrived(c_part(d, i), cs.at[d, i - 1], cr.at[d, i - 1], (up_z, down_z)[d])
+            if i < H:
+                c_send(d, i + 1)
+        for d in range(2):
+            arrived(w_part(d, i), ws.at[d, i - 1], wr.at[d, i - 1], (up_z, down_z)[d])
+            if i < H:
+                w_send(d, i + 1)
+        while i >= 3 and moved < min(2 * i + 1, Z):
+            wx_send(moved)
+            moved += 1
+        if 2 <= i < 2 + NCH:
+            pages_pass(i - 2)
+        for _ in range(8 if i >= 7 else 0):
+            if projected < min(2 * i + 1, Z):
+                project(projected)
+                projected += 1
+        for _ in range({7: 2, 8: 1}.get(i, 0)):
+            wx_pass(passed)
+            passed += 1
         for _ in range(share):
             if work:
                 work.pop(0)()
-        if i >= NCH + 2:
-            for _ in range(2):
-                wx_pass(passed)
-                passed += 1
+    for chunk in range(max(0, H - 1), NCH):
+        pages_pass(chunk)
+    while projected < Z:
+        project(projected)
+        projected += 1
+    project(0)
     while passed < Z:
         wx_pass(passed)
         passed += 1
-    project(0)
     for k in range(1, Z):
         arrived(rp_of(zmod(2 * z - z_of(k))), pjs.at[k - 1], pjr.at[k - 1], up_z)
 
@@ -469,6 +479,7 @@
     H = Z // 2
     smem = pl.BlockSpec(memory_space=pltpu.SMEM)
     vmem = pl.BlockSpec(memory_space=pltpu.VMEM)
+    hbm = pl.BlockSpec(memory_space=pl.ANY)
     tokens = REQ * SPAN
     cols = out_weight.shape[1] * R // T
     V = pltpu.VMEM
@@ -476,9 +487,15 @@
     return pl.pallas_call(
         functools.partial(kernel, Z, T),
         out_shape=jax.ShapeDtypeStruct((tokens, cols), BF16),
-        in_specs=[smem] * 4 + [vmem] * 13,
+        in_specs=[smem] * 4 + [vmem] * 5 + [hbm] * 3 + [vmem] + [hbm] * 2 + [vmem] * 2,
         out_specs=vmem,
         scratch_shapes=[
+            V((tokens, WIDTH), BF16),
+            V((tokens, WIDTH), BF16),
+            V((tokens, N), BF16),
+            V((MISS * tokens, WIDTH), BF16),
+            V((MISS * tokens, N), BF16),
+            D((5,)),
             pltpu.SMEM((16, 2 * R), jnp.int32),
             pltpu.SMEM((PAGES, 2 * R), jnp.int32),
             V((16, 2 * R), jnp.int32),

time: 140 us -> 130 us (0.929)
  Pallas kernels: 138 us -> 128 us
    pallas_call x1, Pallas kernels: 138 us -> 128 us  [per_device(): pl.pallas_call(functools.partial(kernel, Z, T), out_shape=jax.ShapeDtypeS...]
where the time goes in v4:
time: 130 us
  Pallas kernels  128 us (98%)
  local copies, waits for them, and re-layouts  1.67 us (1%)
    pallas_call x1, Pallas kernels, per_device(): pl.pallas_call(functools.partial(kernel, Z, T), out_shape=jax.ShapeDtypeS...  128 us

profile of v4, /device:TPU:1, one launch (start us, length us, event | category | flops | bytes accessed | tf_op | source)
XLA Modules:
  0.0 129.8 jit_solution(4422949456220896737)
XLA Ops:
  0.0 128.1 %shard_map.163 = bf16[256,512]{1,0:T(8,128)(2,1)} custom-call(s32[2]{0:T(128)} %missed.1, f32[16]{0:T(128)} %bias.1, f32[16]{0:T(128)} %a_log.1, f32[16]{0:T(128)} %skip.1, s32[32,1,128]{2,1,0:T(1,128)} %bitcast.12, s32[32,128]{1,0:T(8,128)} %bitcast.13, f32[16,256]{1,0:T(8,128)} %bitcast.14, f32[16,768]{1,0:T(8,128)} %bitcast.11, f32[1,1024]{1,0:T(1,128)} %bitcast.15, ...), custom_call_target="tpu_custom_call" | custom-call | flops 4000000000 | bytes 8000000 | tf_op jit(solution)/shard_map/pallas_call | solution.py:487
  128.1 1.7 %copy.19 = bf16[256,512]{1,0:T(8,128)(2,1)} copy(bf16[256,512]{1,0:T(8,128)(2,1)} %shard_map.163) | data formatting | bytes 524288

commit v5 on v4

--- a/solution.py
+++ b/solution.py
@@ -47,7 +47,7 @@
     missed, bias, a_log, skip, holders, slots, sdt, mdt, gain,
     sx_in, sz_in, sb_in, sc, mx_in, mb_in, w_ref, cache,
     out_ref,
-    sx, sz, sb, mx, mb, load_sems, tables, places, tables_v, places_v, table_sems, wt, cg, outp, pg, relay, sp, rp, pt, a0, a1, xs, qs, skips, hid,
+    sx, sz, sb, mx, mb, load_sems, tables, places, tables_v, places_v, table_sems, wt, cg, outp, pg, relay, sp, rp, pt, a0, a1, xs, qs, skips, hid, mid, mids, midr,
     cs, cr, ws, wr, wxs, wxr, wfs, wfr, pgs, pgr, pjs, pjr,
     xsend, xrecv, ysend, yrecv, coresem_s, coresem_r, ys_s, ys_r,
 ):
@@ -272,9 +272,23 @@
         products = jnp.stack(parts).astype(BF16)
         if k == 0:
             rp[pl.ds(z * 2 * X, 2 * X)] = products
+        elif k == Z - 1:
+            sp[k - 1] = products
+            send(sp.at[k - 1, pl.ds(0, X)], mid.at[0], mids.at[0], midr.at[0], at(x, z - H // 2))
+            send(sp.at[k - 1, pl.ds(X, X)], mid.at[1], mids.at[1], midr.at[1], at(x, z + H // 2))
         else:
             sp[k - 1] = products
             send(sp.at[k - 1], rp_of(z), pjs.at[k - 1], pjr.at[k - 1], at(x, dz))
+
+    def rp_half(zz, d):
+        return rp.at[pl.ds(zmod(zz) * 2 * X + d * X, X)]
+
+    def far_pass():
+        below, above = at(x, z - H // 2), at(x, z + H // 2)
+        arrived(mid.at[0], mids.at[0], midr.at[0], below)
+        send(mid.at[0], rp_half(z + H // 2, 0), mids.at[2], midr.at[2], below)
+        arrived(mid.at[1], mids.at[1], midr.at[1], above)
+        send(mid.at[1], rp_half(z - H // 2, 1), mids.at[3], midr.at[3], above)
 
     lane = iota((1, SPAN), 1)
     lane_block = (lane // HEADS) % 4
@@ -378,8 +392,10 @@
             moved += 1
         if 2 <= i < 2 + NCH:
             pages_pass(i - 2)
-        for _ in range(8 if i >= 7 else 0):
-            if projected < min(2 * i + 1, Z):
+        if i == H:
+            project(Z - 1)
+        for _ in range(8 if i >= H - 1 else 0):
+            if projected < min(2 * i + 1, Z - 1):
                 project(projected)
                 projected += 1
         for _ in range({7: 2, 8: 1}.get(i, 0)):
@@ -390,14 +406,18 @@
                 work.pop(0)()
     for chunk in range(max(0, H - 1), NCH):
         pages_pass(chunk)
-    while projected < Z:
+    while projected < Z - 1:
         project(projected)
         projected += 1
     project(0)
     while passed < Z:
+        if passed == 6:
+            far_pass()
         wx_pass(passed)
         passed += 1
-    for k in range(1, Z):
+    for d in range(2):
+        arrived(rp_half(z + H, d), mids.at[2 + d], midr.at[2 + d], up_z)
+    for k in range(1, Z - 1):
         arrived(rp_of(zmod(2 * z - z_of(k))), pjs.at[k - 1], pjr.at[k - 1], up_z)
 
     eye = (iota((SPAN, SPAN), 0) == iota((SPAN, SPAN), 1)).astype(BF16)
@@ -430,17 +450,20 @@
         def block_of(k, core):
             return lax.rem(y + offsets[k], Y) * 2 + core
 
-        for k in range(4):
+        def give(k):
             xsend[k] = product(block_of(k, 1 - c)).astype(BF16)
             send(xsend.at[k], xrecv.at[k], coresem_s.at[k], coresem_r.at[k], other)
 
         def both(k):
+            if k < 3:
+                give(k + 1)
             mine = product(block_of(k, c))
             arrived(xrecv.at[k], coresem_s.at[k], coresem_r.at[k], other)
             return mine + xrecv[k].astype(F32)
 
         half = out_ref.shape[0] // 2
         lo, hi = pl.ds(0, half), pl.ds(half, half)
+        give(0)
         ysend[0] = both(0).astype(BF16)
         send(ysend.at[0, lo], yrecv.at[0], ys_s.at[0], ys_r.at[0], y_up)
         send(ysend.at[0, hi], yrecv.at[1], ys_s.at[1], ys_r.at[1], y_down)
@@ -515,6 +538,8 @@
             V((6, SPAN, SPAN), F32),
             V((8, WIDTH), F32),
             V((tokens, WIDTH), BF16),
+            V((2, X, ROWS, SPAN), BF16),
+            D((4,)), D((4,)),
             D((2, H)), D((2, H)), D((2, H)), D((2, H)),
             D((2, Z)), D((2, Z)), D((2, Z)), D((2, Z)),
             D((NCH, 6)), D((NCH, 6)), D((Z - 1,)), D((Z - 1,)),

time: 130 us -> 130 us (level)
  no operation moved by 1% of the time
where the time goes in v5:
time: 130 us
  Pallas kernels  128 us (98%)
  local copies, waits for them, and re-layouts  1.67 us (1%)
    pallas_call x1, Pallas kernels, per_device(): pl.pallas_call(functools.partial(kernel, Z, T), out_shape=jax.ShapeDtypeS...  128 us

profile of v5, /device:TPU:1, one launch (start us, length us, event | category | flops | bytes accessed | tf_op | source)
XLA Modules:
  0.0 129.9 jit_solution(12529458311137195924)
XLA Ops:
  0.0 128.3 %shard_map.163 = bf16[256,512]{1,0:T(8,128)(2,1)} custom-call(s32[2]{0:T(128)} %missed.1, f32[16]{0:T(128)} %bias.1, f32[16]{0:T(128)} %a_log.1, f32[16]{0:T(128)} %skip.1, s32[32,1,128]{2,1,0:T(1,128)} %bitcast.12, s32[32,128]{1,0:T(8,128)} %bitcast.13, f32[16,256]{1,0:T(8,128)} %bitcast.14, f32[16,768]{1,0:T(8,128)} %bitcast.11, f32[1,1024]{1,0:T(1,128)} %bitcast.15, ...), custom_call_target="tpu_custom_call" | custom-call | flops 4000000000 | bytes 8000000 | tf_op jit(solution)/shard_map/pallas_call | solution.py:510
  128.3 1.7 %copy.19 = bf16[256,512]{1,0:T(8,128)(2,1)} copy(bf16[256,512]{1,0:T(8,128)(2,1)} %shard_map.163) | data formatting | bytes 524288
